TPU v7x, 32 devices: a whole 2x2x4 slice. The times are simulated.
32 devices in a mesh: row: 8 (over z, y), col: 4 (over x, core).
Axes of the slice: x: 2, y: 2, z: 4, core: 2. Of those that a mesh axis runs over, the one named last changes fastest.
Arguments:
- image_tokens: bfloat16 [51200, 768], P(('row', 'col')), may hold values from -9 to 9
- image_norm_gain: float32 [2, 768], replicated, may hold values from 0.5 to 1.5
- image_norm_bias: float32 [2, 768], replicated, may hold values from -1.75 to 1.75
- image_qkv: bfloat16 [768, 2304], P('col'), may hold values from -0.21875 to 0.21875
- image_out: bfloat16 [768, 768], P('col'), may hold values from -0.625 to 0.625
- image_up: bfloat16 [768, 3072], P('col'), may hold values from -0.21875 to 0.21875
- image_down: bfloat16 [3072, 768], P('col'), may hold values from -0.15625 to 0.15625
- text_tokens: bfloat16 [16384, 768], P(('row', 'col')), may hold values from -6 to 6
- text_lengths: int32 [1024], P(('row', 'col')), may hold values from 4 to 16, as said below
- norm1_gain: float32 [768], replicated, may hold values from 0.5 to 1.5
- norm1_bias: float32 [768], replicated, may hold values from -1.75 to 1.75
- norm2_gain: float32 [768], replicated, may hold values from 0.5 to 1.5
- norm2_bias: float32 [768], replicated, may hold values from -1.75 to 1.75
- text_qkv: bfloat16 [768, 2304], replicated, may hold values from -0.21875 to 0.21875
- text_out: bfloat16 [768, 768], replicated, may hold values from -0.625 to 0.625
- text_up: bfloat16 [768, 3072], replicated, may hold values from -0.21875 to 0.21875
- text_down: bfloat16 [3072, 768], replicated, may hold values from -0.15625 to 0.15625
- text_proj: bfloat16 [768, 768], replicated, may hold values from -0.21875 to 0.21875
Outputs:
- mean_loss: float32 [], replicated
- text_hidden: bfloat16 [16384, 768], P(('row', 'col'))
- text_input_grad: bfloat16 [16384, 768], P(('row', 'col'))
- grad_norm1_gain: float32 [768], replicated
- grad_norm1_bias: float32 [768], replicated
- grad_norm2_gain: float32 [768], replicated
- grad_norm2_bias: float32 [768], replicated
- grad_qkv: float32 [768, 2304], P('row', 'col')
- grad_out: float32 [768, 768], P('row', 'col')
- grad_up: float32 [768, 3072], P('row', 'col')
- grad_down: float32 [3072, 768], P('row', 'col')
- grad_proj: float32 [768, 768], P('row', 'col')
Inputs may be any that keep to these rules, and one draw needn't show every extreme that they name: Caption n's true tokens are its first text_lengths[n] slots; some caption has 16 and some has 4.
All inputs are finite; a program needn't handle non-finite values.
Results may differ from a plain program's by a relative error of at most 0.015.
Values may be sent and summed in bfloat16 or wider, within the bound.
A program may use at most 256 MiB of HBM per device.

v0:
```python
import functools
import math
from types import SimpleNamespace

import jax
import jax.numpy as jnp
from jax import lax
from jax.experimental import pallas as pl
from jax.experimental.pallas import tpu as pltpu
from jax.sharding import PartitionSpec as P

HEADS = 12
IMG_TOK = 50
norm_eps = 1e-06
logit_scale = 50.0
masked_score = -1e30
log2e = math.log2(math.e)
f32 = jnp.float32
bf16 = jnp.bfloat16
VMEM_LIMIT = 62 * 2**20
MESH = pl.DeviceIdType.MESH


def dot_nn(a, b):
    return lax.dot_general(a, b, (((1,), (0,)), ((), ())), preferred_element_type=f32)


def dot_nt(a, b):
    return lax.dot_general(a, b, (((1,), (1,)), ((), ())), preferred_element_type=f32)


def dot_tn(a, b):
    return lax.dot_general(a, b, (((0,), (0,)), ((), ())), preferred_element_type=f32)


def split_low(x):
    high = x.astype(bf16)
    return high, (x - high.astype(f32)).astype(bf16)


def normed(x):
    centered = x - jnp.mean(x, axis=-1, keepdims=True)
    spread = lax.rsqrt(jnp.mean(centered * centered, axis=-1, keepdims=True) + norm_eps)
    return centered * spread, spread


def layer_norm(x, gain, bias):
    return normed(x)[0] * gain + bias


def gelu(x):
    return x * (0.5 + 0.5 * lax.erf(x * math.sqrt(0.5)))


def gelu_and_slope(x):
    below = 0.5 + 0.5 * lax.erf(x * math.sqrt(0.5))
    bell = jnp.exp2((-0.5 * log2e) * (x * x))
    return x * below, below + x * (bell * (1.0 / math.sqrt(2.0 * math.pi)))


def lane_halves(width):
    lane = lax.broadcasted_iota(jnp.int32, (1, width), 1)
    first = (lane < width // 2).astype(f32)
    return first.astype(bf16), (1.0 - first).astype(bf16)


def stack_heads(x, first, second):
    return jnp.concatenate([x * first, x * second], axis=0)


def join_heads(stacked):
    rows, width = stacked.shape[0] // 2, stacked.shape[1]
    lane = lax.broadcasted_iota(jnp.int32, (rows, width), 1)
    return jnp.where(lane < width // 2, stacked[:rows], stacked[rows:])


def soft_weights(query, key, bias, factor):
    scores = dot_nt(query, key) * (factor * log2e) + bias
    weights = jnp.exp2(scores - jnp.max(scores, axis=-1, keepdims=True))
    return weights, 1.0 / jnp.sum(weights, axis=-1, keepdims=True)


def set_lengths(lengths_ref, lens_ref, key_bias_ref):
    captions, tokens = lens_ref.shape[0], key_bias_ref.shape[1]
    length = tokens // captions
    caption = lax.broadcasted_iota(jnp.int32, (captions, 1), 0)
    token = lax.broadcasted_iota(jnp.int32, (1, tokens), 1)
    column, row = jnp.zeros((captions, 1), jnp.int32), jnp.zeros((1, tokens), jnp.int32)
    for n in range(captions):
        column = jnp.where(caption == n, lengths_ref[n], column)
        row = jnp.where(token // length == n, lengths_ref[n], row)
    lens_ref[...] = column
    key_bias_ref[...] = jnp.where(token % length < row, 0.0, masked_score)


def as_row(ref):
    return ref[...].reshape(1, ref.shape[0])


def text_bias(key_bias_ref, block, rows, length):
    near = lax.broadcasted_iota(jnp.int32, (rows, rows), 0) // length
    far = lax.broadcasted_iota(jnp.int32, (rows, rows), 1) // length
    columns = pl.ds(pl.multiple_of(block * rows, rows), rows)
    bias = jnp.where(near == far, key_bias_ref[:, columns], masked_score)
    return jnp.concatenate([bias, bias], axis=0)


def member(len_ref, captions, tokens):
    length = tokens // captions
    token = lax.broadcasted_iota(jnp.int32, (captions, tokens), 1)
    caption = lax.broadcasted_iota(jnp.int32, (captions, tokens), 0)
    return ((token // length == caption) & (token % length < len_ref[...])).astype(f32)


def spread_rows(x, length):
    rows, width = x.shape
    return jnp.broadcast_to(x[:, None, :], (rows, length, width)).reshape(rows * length, width)


def wide_steps(total, most=768):
    step = math.gcd(total, most)

    def loop(body):
        @pl.loop(0, total // step)
        def _(j):
            body(pl.ds(pl.multiple_of(j * step, 128), step))

    return loop


class TextForward:
    band = 128

    def __init__(self, refs):
        for name, ref in refs.items():
            setattr(self, name, ref)
        self.tokens, self.width = self.tok.shape
        self.captions = self.lens.shape[0]
        self.length = self.tokens // self.captions
        self.wide = self.w_up.shape[1]
        pairs = (
            (self.qkv_hbm, self.w_qkv), (self.out_hbm, self.w_out), (self.up_hbm, self.w_up),
            (self.down_hbm, self.w_down),
        )
        self.loads = load_weights(pairs, self.sems)
        self.load_proj = pltpu.make_async_copy(self.proj_hbm, self.w_proj, self.sems.at[4])

    def bands(self, step):
        pl.loop(0, self.tokens // self.band)(
            lambda i: step(pl.ds(pl.multiple_of(i * self.band, self.band), self.band))
        )

    def prepare(self):
        set_lengths(self.lengths, self.lens, self.key_bias)

        def first_norm(rows):
            norm = layer_norm(self.tok[rows, :].astype(f32), as_row(self.gain1), as_row(self.bias1))
            self.norm[rows, :] = norm.astype(bf16)

        self.bands(first_norm)

    def attention(self):
        width = self.width
        self.loads[0].wait()

        @wide_steps(3 * width)
        def _(columns):
            self.heads[:, columns] = dot_nn(self.norm[...], self.w_qkv[:, columns]).astype(bf16)

        first, second = lane_halves(128)
        factor = (width // HEADS) ** -0.5

        @pl.loop(0, self.tokens // self.band)
        def _(block):
            rows = pl.ds(pl.multiple_of(block * self.band, self.band), self.band)
            bias = text_bias(self.key_bias, block, self.band, self.length)
            for at in range(0, width, 128):
                query = stack_heads(self.heads[rows, at : at + 128], first, second)
                key = self.heads[rows, width + at : width + at + 128]
                weights, scale = soft_weights(query, key, bias, factor)
                value = self.heads[rows, 2 * width + at : 2 * width + at + 128]
                mixed = dot_nn(weights.astype(bf16), value) * scale
                self.mixed[rows, at : at + 128] = join_heads(mixed).astype(bf16)

    def middle(self):
        self.loads[1].wait()

        def second_norm(rows):
            mid = self.tok[rows, :].astype(f32) + dot_nn(self.mixed[rows, :], self.w_out[...])
            self.mid[rows, :] = mid
            self.norm[rows, :] = layer_norm(mid, as_row(self.gain2), as_row(self.bias2)).astype(bf16)

        self.bands(second_norm)

    def feed(self, after=lambda j: None):
        self.loads[2].wait()
        self.chosen = member(self.lens, self.captions, self.tokens).astype(bf16)
        place = lax.broadcasted_iota(jnp.int32, (self.captions, self.length, 1), 1)
        valid = (place < self.lens[...].reshape(self.captions, 1, 1)).astype(f32).reshape(self.tokens, 1)

        @pl.loop(0, self.wide // self.width)
        def _(j):
            columns = pl.ds(pl.multiple_of(j * self.width, 128), self.width)
            value, slope = gelu_and_slope(dot_nn(self.norm[...], self.w_up[:, columns]))
            value = value.astype(bf16)
            self.inner[:, columns] = value
            self.slope[:, columns] = (slope * valid).astype(bf16)
            self.inner_sum[:, columns] = dot_nn(self.chosen, value).astype(bf16)
            after(j)

    def finish(self):
        self.loads[3].wait()
        self.turned[...] = self.norm[...].T
        inverse = 1.0 / self.lens[...].astype(f32)

        @wide_steps(self.width)
        def _(columns):
            state = self.mid[:, columns] + dot_nn(self.inner[...], self.w_down[:, columns])
            self.hidden[:, columns] = state.astype(bf16)
            high, low = split_low(state)
            pooled = (dot_nn(self.chosen, high) + dot_nn(self.chosen, low)) * inverse
            self.pooled[:, columns] = pooled.astype(bf16)

    def embed(self):
        self.load_proj.wait()
        projected = dot_nn(self.pooled[...], self.w_proj[...])
        self.projected[...] = projected
        scale = lax.rsqrt(jnp.sum(projected * projected, axis=-1, keepdims=True) + norm_eps)
        self.text_embed[...] = (projected * scale).astype(bf16)


text_ins = (
    "tok", "lengths", "gain1", "bias1", "gain2", "bias2", "qkv_hbm", "out_hbm", "up_hbm", "down_hbm", "proj_hbm",
)
text_names = (
    "hidden", "text_embed", "projected", "pooled", "inner_sum", "heads", "mixed", "mid", "slope", "turned",
)
text_scratch = ("w_qkv", "w_out", "w_up", "w_down", "w_proj", "norm", "inner", "lens", "key_bias", "sems")


def text_forward_kernel(*refs):
    t = TextForward(dict(zip(text_ins + text_names + text_scratch, refs, strict=True)))
    t.load_proj.start()
    t.prepare()
    t.attention()
    t.middle()
    t.feed()
    t.finish()
    t.embed()


def load_weights(pairs, sems):
    loads = [pltpu.make_async_copy(s, d, sems.at[i]) for i, (s, d) in enumerate(pairs)]
    for load in loads:
        load.start()
    return loads


def spans(count, size):
    return lambda i: pl.ds(pl.multiple_of(i * size, size), size)


def norm_backward(outer, unit, spread, gain):
    outer = outer * gain
    inner = outer - jnp.mean(outer, axis=-1, keepdims=True)
    return spread * (inner - unit * jnp.mean(outer * unit, axis=-1, keepdims=True))


class TextBackward:
    band = 128

    def __init__(self, refs, loads):
        for name, ref in refs.items():
            setattr(self, name, ref)
        self.loads = loads
        self.tokens, self.width = self.tok.shape
        self.captions = self.lens.shape[0]
        self.length = self.tokens // self.captions
        self.wide = self.w_up.shape[1]
        self.pre_grad = self.slope

    def wait(self, name):
        if name in self.loads:
            self.loads[name].wait()

    def rows(self, i):
        return pl.ds(pl.multiple_of(i * self.band, self.band), self.band)

    def bands(self, step):
        pl.loop(0, self.tokens // self.band)(lambda i: step(self.rows(i)))

    def valid(self):
        place = lax.broadcasted_iota(jnp.int32, (self.captions, self.length, 1), 1)
        valid = place < self.lens[...].reshape(self.captions, 1, 1)
        return valid.astype(f32).reshape(self.tokens, 1)

    def project(self):
        projected = self.projected[...]
        embed_grad = self.embed_grad[...]
        r = lax.rsqrt(jnp.sum(projected * projected, axis=-1, keepdims=True) + norm_eps)
        along = jnp.sum(projected * embed_grad, axis=-1, keepdims=True)
        proj_grad = (r * embed_grad - (r * r * r) * projected * along).astype(bf16)
        self.wait("w_proj")
        state_grad = dot_nt(proj_grad, self.w_proj[...]) * (1.0 / self.lens[...].astype(f32))
        self.branch[...] = state_grad.astype(bf16)
        self.mid_grad[...] = spread_rows(state_grad, self.length) * self.valid()
        return proj_grad, self.branch[...]

    def wait_inner(self):
        self.wait("turned")
        self.wait("w_down")
        self.wait("slope")

    def inner_grad(self, columns):
        grad = dot_nt(self.branch[...], self.w_down[columns, :])
        pre_grad = spread_rows(grad, self.length) * self.slope[:, columns].astype(f32)
        self.pre_grad[:, columns] = pre_grad.astype(bf16)

    def up_block(self, columns):
        return dot_nn(self.turned[...], self.pre_grad[:, columns]).astype(bf16)

    def to_middle(self):
        self.wait("w_up")

        @wide_steps(self.width)
        def _(columns):
            self.outer[:, columns] = dot_nt(self.pre_grad[...], self.w_up[columns, :])

    def middle(self):
        self.wait("mid")
        self.norm_grad[...] = jnp.zeros_like(self.norm_grad)

        def through_norm(rows):
            unit, spread = normed(self.mid[rows, :])
            outer = self.outer[rows, :]
            self.norm_grad[2:3, :] += jnp.sum(outer * unit, axis=0, keepdims=True)
            self.norm_grad[3:4, :] += jnp.sum(outer, axis=0, keepdims=True)
            mid_grad = self.mid_grad[rows, :] + norm_backward(outer, unit, spread, as_row(self.gain2))
            self.mid_grad[rows, :] = mid_grad
            self.low_grad[rows, :] = mid_grad.astype(bf16)

        self.bands(through_norm)
        self.wait("mixed")
        self.turned[...] = self.mixed[...].T

    def out_block(self, columns):
        return dot_nn(self.turned[...], self.low_grad[:, columns]).astype(bf16)

    def to_heads(self):
        self.wait("w_out")
        self.wait("tok")

        def through_out(rows):
            self.mixed_grad[rows, :] = dot_nt(self.low_grad[rows, :], self.w_out[...]).astype(bf16)
            norm = layer_norm(self.tok[rows, :].astype(f32), as_row(self.gain1), as_row(self.bias1))
            self.norm[rows, :] = norm.astype(bf16)

        self.bands(through_out)
        self.turned[...] = self.norm[...].T

    def attention(self, after=lambda block: None):
        first, second = lane_halves(128)
        width = self.width
        factor = (width // HEADS) ** -0.5
        self.wait("heads")
        self.key_column[...] = jnp.broadcast_to((1.0 - self.valid()) * masked_score, self.key_column.shape)

        @pl.loop(0, self.tokens // self.band)
        def _(block):
            rows = self.rows(block)
            near = lax.broadcasted_iota(jnp.int32, (self.band, self.band), 0) // self.length
            far = lax.broadcasted_iota(jnp.int32, (self.band, self.band), 1) // self.length
            bias = jnp.where(near == far, self.key_column[rows, :], masked_score)
            bias = jnp.concatenate([bias, bias], axis=1)
            for at in range(0, width, 128):
                query = stack_heads(self.heads[rows, at : at + 128], first, second)
                key = self.heads[rows, width + at : width + at + 128]
                value = self.heads[rows, 2 * width + at : 2 * width + at + 128]
                grad = stack_heads(self.mixed_grad[rows, at : at + 128], first, second)
                scores = dot_nt(key, query) * (factor * log2e) + bias
                weights = jnp.exp2(scores - jnp.max(scores, axis=0, keepdims=True))
                probs = weights * (1.0 / jnp.sum(weights, axis=0, keepdims=True))
                prob_grad = dot_nt(value, grad)
                total = jnp.sum(prob_grad * probs, axis=0, keepdims=True)
                score_grad = (probs * (prob_grad - total)).astype(bf16)
                query_grad = join_heads(dot_tn(score_grad, key)) * factor
                self.heads_grad[rows, at : at + 128] = query_grad.astype(bf16)
                key_grad = dot_nn(score_grad, query) * factor
                self.heads_grad[rows, width + at : width + at + 128] = key_grad.astype(bf16)
                value_grad = dot_nn(probs.astype(bf16), grad)
                self.heads_grad[rows, 2 * width + at : 2 * width + at + 128] = value_grad.astype(bf16)
            after(block)

    def qkv_block(self, columns):
        return dot_nn(self.turned[...], self.heads_grad[:, columns]).astype(bf16)

    def input(self, between=lambda: None):
        self.wait("w_qkv")

        @wide_steps(self.width)
        def _(columns):
            self.outer[:, columns] = dot_nt(self.heads_grad[...], self.w_qkv[columns, :])

        between()

        def through_norm(rows):
            unit, spread = normed(self.tok[rows, :].astype(f32))
            outer = self.outer[rows, :]
            self.norm_grad[0:1, :] += jnp.sum(outer * unit, axis=0, keepdims=True)
            self.norm_grad[1:2, :] += jnp.sum(outer, axis=0, keepdims=True)
            inner = norm_backward(outer, unit, spread, as_row(self.gain1))
            self.tok[rows, :] = (self.mid_grad[rows, :] + inner).astype(bf16)

        self.bands(through_norm)


backward_ins = (
    "lengths", "gain1", "bias1", "gain2", "bias2", "embed_grad", "projected", "tok_hbm", "heads_hbm", "mixed_hbm",
    "mid_hbm", "slope_hbm", "turned_hbm", "w_qkv_hbm", "w_out_hbm", "w_up_hbm", "w_down_hbm", "w_proj_hbm",
)
backward_outs = ("proj_grad", "branch", "up_grad", "out_grad", "qkv_grad", "input_grad", "norm_grad")
backward_scratch = (
    "tok", "heads", "mixed", "mid", "slope", "w_qkv", "w_out", "w_up", "w_down", "w_proj", "norm", "turned",
    "outer", "mid_grad", "low_grad", "mixed_grad", "heads_grad", "lens", "key_bias", "key_column", "sems",
)


def text_backward_kernel(*refs):
    refs = dict(zip(backward_ins + backward_outs + backward_scratch, refs, strict=True))
    order = ("w_proj", "turned", "w_down", "slope", "w_up", "mid", "mixed", "w_out", "tok", "heads", "w_qkv")
    loads = load_weights([(refs[name + "_hbm"], refs[name]) for name in order], refs["sems"])
    t = TextBackward(refs, dict(zip(order, loads)))
    set_lengths(t.lengths, t.lens, t.key_bias)
    parts = t.up_grad.shape[0]

    def blocks(target, block):
        step = target.shape[2]
        for part in range(parts):
            target[part] = block(slice(part * step, (part + 1) * step))

    t.proj_grad[...] = t.project()[0]
    t.wait_inner()
    wide_steps(t.wide)(t.inner_grad)
    blocks(t.up_grad, t.up_block)
    t.to_middle()
    t.middle()
    blocks(t.out_grad, t.out_block)
    t.to_heads()
    t.attention()
    blocks(t.qkv_grad, t.qkv_block)
    t.input()
    t.input_grad[...] = t.tok[...]


class Place:
    def __init__(self, z_count=4, y_count=2, x_count=2, k_count=2):
        self.row, self.col = lax.axis_index("row"), lax.axis_index("col")
        self.z, self.y = self.row // y_count, self.row % y_count
        self.x, self.k = self.col // k_count, self.col % k_count
        self.rows, self.cols = z_count * y_count, x_count * k_count
        self.count = self.rows * self.cols
        self.me = self.row * self.cols + self.col
        self.slot = self.col * self.rows + self.row
        self.near_z, self.far_z = self.z + 1 - 2 * (self.z % 2), (self.z + 2) % 4

    def at(self, **moved):
        z, y, x, k = (moved.get(name, getattr(self, name)) for name in "zyxk")
        return z * 2 + y, x * 2 + k

    def peer(self, distance):
        other = (self.me + distance) % self.count
        return other // self.cols, other % self.cols

    def greet(self):
        barrier = pltpu.get_barrier_semaphore()

        @pl.loop(1, self.count)
        def _(distance):
            pl.semaphore_signal(barrier, inc=1, device_id=self.peer(distance), device_id_type=MESH)

    def meet(self):
        pl.semaphore_wait(pltpu.get_barrier_semaphore(), self.count - 1)


def remote(src, dst, send, recv, to):
    return pltpu.make_async_remote_copy(
        src_ref=src, dst_ref=dst, send_sem=send, recv_sem=recv, device_id=to, device_id_type=MESH
    )


def wait_all(blocks, send, recv, to):
    remote(blocks, blocks, send, recv, to).wait()


class Gather:
    def __init__(self, place, pieces, spans, sends, recvs):
        mate, next_x = place.at(k=1 - place.k), place.at(x=1 - place.x)
        across = next_x[1]
        self.spans, self.sends, self.recvs, self.mate = spans, sends, recvs, mate
        self.locals, self.nears, self.fars, self.alongs, self.passes = [], [], [], [], []
        for axis, own, half, block, part in pieces:
            here = place.y if axis == "y" else place.z % 2
            partner = place.at(y=1 - place.y) if axis == "y" else place.at(z=place.near_z)
            mine, theirs = part(across, here), block(across)
            self.locals.append(pltpu.make_async_copy(own, block(place.col), recvs.at[4]))
            self.nears.append(remote(own, block(place.col), sends.at[0], recvs.at[0], mate))
            self.fars.append(remote(half(here), part(place.col, here), sends.at[1], recvs.at[1], next_x))
            self.alongs.append(remote(mine, mine, sends.at[2], recvs.at[2], partner))
            self.passes.append(remote(theirs, theirs, sends.at[3], recvs.at[3], mate))

    def wait(self, i, span):
        wait_all(self.spans[span], self.sends.at[i], self.recvs.at[i], self.mate)

    def start(self):
        for copies in (self.fars, self.nears, self.locals):
            for copy in copies:
                copy.start()

    def share(self):
        self.wait(1, 1)
        for copy in self.alongs:
            copy.start()

    def relay(self):
        self.wait(2, 1)
        for copy in self.passes:
            copy.start()

    def finish(self):
        pltpu.make_async_copy(self.spans[0], self.spans[0], self.recvs.at[4]).wait()
        self.wait(0, 0)
        self.wait(3, 0)


class RowFactors:
    def __init__(self, place, own, held, local, sends, recvs):
        self.place, self.own, self.held, self.sends, self.recvs = place, own, held, sends, recvs
        self.local = pltpu.make_async_copy(own.at[place.row], held.at[place.col, place.row], local)
        mine, across = held.at[place.col], held.at[place.at(x=1 - place.x)[1]]
        mate, next_x = place.at(k=1 - place.k), place.at(x=1 - place.x)
        self.far = remote(mine, mine, sends.at[1], recvs.at[1], next_x)
        self.near = remote(mine, mine, sends.at[2], recvs.at[2], mate)
        self.passed = remote(across, across, sends.at[3], recvs.at[3], mate)

    def start(self):
        self.local.start()
        p = self.place

        @pl.loop(1, p.rows)
        def _(distance):
            row = (p.row + distance) % p.rows
            remote(
                self.own.at[row], self.held.at[p.col, p.row], self.sends.at[0], self.recvs.at[0], (row, p.col)
            ).start()

    def share(self):
        self.local.wait()
        p = self.place
        to = p.at(k=1 - p.k)
        wait_all(self.held.at[p.col, pl.ds(0, p.rows - 1)], self.sends.at[0], self.recvs.at[0], to)
        self.far.start()
        self.near.start()

    def relay(self):
        self.far.wait()
        self.passed.start()

    def finish(self):
        self.near.wait()
        self.passed.wait()


class Exchange:
    def __init__(self, place, source, slots, sends, recvs):
        self.place, self.source, self.slots = place, source, slots
        self.sems = sends.at[0], recvs.at[0]

    def start(self):
        p = self.place

        @pl.loop(1, p.count)
        def _(distance):
            remote(self.source, self.slots.at[p.slot], *self.sems, p.peer(distance)).start()

    def finish(self):
        p = self.place
        wait_all(self.slots.at[pl.ds(0, p.count - 1)], *self.sems, p.at(k=1 - p.k))


class ChipSum:
    def __init__(self, place, total, got, slots, sends, recvs):
        self.place, self.total, self.got, self.slots = place, total, got, slots
        self.sends, self.recvs = sends, recvs
        self.chip, self.chips = place.row * 2 + place.x, place.rows * 2
        self.mate = place.at(k=1 - place.k)

    def near(self):
        return remote(self.total, self.got, self.sends.at[0], self.recvs.at[0], self.mate)

    def start(self):
        self.near().start()

    def spread(self):
        self.near().wait()
        self.total[...] = self.total[...] + self.got[...]
        self.slots[self.chip] = self.total[...]

        @pl.loop(1, self.chips)
        def _(distance):
            other = (self.chip + distance) % self.chips
            to = other // 2, other % 2 * 2 + self.place.k
            remote(self.total, self.slots.at[self.chip], self.sends.at[1], self.recvs.at[1], to).start()

    def finish(self):
        wait_all(self.slots.at[pl.ds(0, self.chips - 1)], self.sends.at[1], self.recvs.at[1], self.mate)
        return jnp.sum(self.slots[...], axis=0)


class GradientScatter:
    def __init__(self, place, straight, halves, held, near, x1, y1, x2, y2, far, sends, recvs):
        self.straight = straight
        self.place, self.held, self.near, self.far = place, held, near, far
        self.x1, self.y1, self.x2, self.y2 = x1, y1, x2, y2
        self.sends, self.recvs = sends, recvs
        self.halves = halves

    def lanes(self, chunk):
        ones, twos = zip(*self.halves[:chunk], (0, 0))
        at_one, at_two = sum(ones), sum(twos)
        at = at_one + at_two
        one, two = self.halves[chunk]
        return (
            pl.ds(at, one + two), pl.ds(at, one), pl.ds(at + one, two), pl.ds(at_one, one), pl.ds(at_two, two)
        )

    def copies(self, chunk, stage):
        p, held = self.place, self.held
        x, y, z, k = p.x, p.y, p.z, p.k
        whole, one, two, part_one, part_two = self.lanes(chunk)

        def copy(n, src, dst, **moved):
            send = self.sends.at[chunk, (0, 0, 1, 0, 1, 0, 1, 2)[n]]
            return remote(src, dst, send, self.recvs.at[chunk, n], p.at(**moved))

        if stage == 0:
            return [copy(0, held.at[:, 1 - k, :, :, :, whole], self.near.at[:, :, :, :, whole], k=1 - k)]
        if stage == 1:
            copies = []
            if one.size:
                copies.append(copy(1, held.at[1 - x, k, :, :, :, one], self.x1.at[:, :, :, part_one], x=1 - x))
            if two.size:
                copies.append(copy(2, held.at[:, k, :, 1 - y, :, two], self.y1.at[:, :, :, part_two], y=1 - y))
            return copies
        if stage == 2:
            copies = []
            if one.size:
                copies.append(copy(3, held.at[x, k, :, 1 - y, :, one], self.y2.at[:, :, part_one], y=1 - y))
            if two.size:
                copies.append(copy(4, held.at[1 - x, k, :, y, :, two], self.x2.at[:, :, part_two], x=1 - x))
            return copies
        if stage == 3 and self.straight:
            return [
                copy(4 + i, held.at[x, k, (z + i) % 4, y, :, whole], self.far.at[i - 1, :, whole], z=(z + i) % 4)
                for i in range(1, 4)
            ]
        if stage == 3:
            blocks = p.near_z, held.shape[2] - 1 - z
            return [
                copy(5 + i, held.at[x, k, block, y, :, whole], self.far.at[i, :, whole], z=p.near_z)
                for i, block in enumerate(blocks)
            ]
        return [copy(7, held.at[x, k, p.far_z, y, :, whole], self.far.at[2, :, whole], z=p.far_z)]

    def start(self, chunk, stage):
        for copy in self.copies(chunk, stage):
            copy.start()

    def finish(self, chunk, stage):
        for copy in self.copies(chunk, stage):
            copy.wait()
        p, held = self.place, self.held
        x, y, k = p.x, p.y, p.k
        z_count = held.shape[2]
        whole, one, two, part_one, part_two = self.lanes(chunk)

        def add(target, source):
            target[...] = (target[...].astype(f32) + source[...].astype(f32)).astype(bf16)

        if stage == 0:

            @pl.loop(0, z_count)
            def _(z):
                for i in range(2):
                    for j in range(2):
                        add(held.at[i, k, z, j, :, whole], self.near.at[i, z, j, :, whole])

        if stage == 1:

            @pl.loop(0, z_count)
            def _(z):
                for i in range(2):
                    if one.size:
                        add(held.at[x, k, z, i, :, one], self.x1.at[z, i, :, part_one])
                    if two.size:
                        add(held.at[i, k, z, y, :, two], self.y1.at[i, z, :, part_two])

        if stage == 2:

            @pl.loop(0, z_count)
            def _(z):
                if one.size:
                    add(held.at[x, k, z, y, :, one], self.y2.at[z, :, part_one])
                if two.size:
                    add(held.at[x, k, z, y, :, two], self.x2.at[z, :, part_two])

        if stage == 3 and not self.straight:
            add(held.at[x, k, p.far_z, y, :, whole], self.far.at[1, :, whole])

    def step_on(self, chunk, stage):
        self.finish(chunk, stage - 1)
        self.start(chunk, stage)

    def total(self):
        p = self.place
        total = self.held[p.x, p.k, p.z, p.y, :, : self.far.shape[2]].astype(f32)
        for i in (0, 1, 2) if self.straight else (0, 2):
            total = total + self.far[i].astype(f32)
        return total


def chip_sum_scratch(size, chips):
    return [
        pltpu.VMEM((1, size), f32), pltpu.VMEM((1, size), f32), pltpu.VMEM((chips, 1, size), f32),
        pltpu.SemaphoreType.DMA((2,)), pltpu.SemaphoreType.DMA((2,)),
    ]


def scatter_scratch(rows, halves):
    one, two = (sum(widths) for widths in zip(*halves))
    spare = max(two, 128)
    shapes = [
        (2, 2, 4, 2, rows, one + two), (2, 4, 2, rows, one + two), (4, 2, rows, one), (2, 4, rows, spare),
        (4, rows, spare), (4, rows, one), (3, rows, one + two),
    ]
    sems = [pltpu.SemaphoreType.DMA((len(halves), 3)), pltpu.SemaphoreType.DMA((len(halves), 8))]
    return [pltpu.VMEM(shape, bf16) for shape in shapes] + sems


class ColFactors:
    def __init__(self, place, own, held, sends, recvs):
        self.place, self.own, self.held, self.sends, self.recvs = place, own, held, sends, recvs

    def copies(self, stage):
        p, held = self.place, self.held

        def copy(n, src, dst, **moved):
            return remote(src, dst, self.sends.at[n], self.recvs.at[n], p.at(**moved))

        if stage == 0:
            mine = held.at[p.col, p.row]
            moves = ({"x": 1 - p.x}, {"k": 1 - p.k}, {"x": 1 - p.x, "k": 1 - p.k})
            return [copy(i, self.own.at[p.at(**move)[1]], mine, **move) for i, move in enumerate(moves)]
        if stage == 1:
            mine = held.at[:, p.row]
            return [copy(3, mine, mine, y=1 - p.y)]
        mine, other = (held.at[:, pl.ds(z * 2, 2)] for z in (p.z, p.far_z))
        if stage == 2:
            return [copy(4, mine, mine, z=p.far_z)]
        return [copy(5, mine, mine, z=p.near_z), copy(6, other, other, z=p.near_z)]

    def start(self, stage):
        for copy in self.copies(stage):
            copy.start()

    def finish(self, stage):
        for copy in self.copies(stage):
            copy.wait()


def scatter_widths(wide, width, cols):
    ups = tuple((128, 128) for _ in range(wide // cols // 256))
    rest = 4 * width // cols - 128
    return ups, ((128, 0),), ((128, 128), (128, 128), (rest - 512, 0))


scatter_names = ("x2", "y2", "far", "sends", "recvs")
total_names = ("total", "got", "slots", "sends", "recvs")


def hand_over_kernel(pair_total, norms, *refs):
    sources, (loss, *vectors), targets = refs[:7], refs[7:12], refs[12:]
    width = vectors[0].shape[0]
    loss[...] = norms[:, 4 * width : 4 * width + 1] * (1.0 / pair_total)
    for i, vector in enumerate(vectors):
        vector[...] = norms[:, i * width : (i + 1) * width].reshape(width)
    for source, target in zip(sources, targets, strict=True):
        target[...] = source[...]


def group_mean(images, rows):
    token = lax.broadcasted_iota(jnp.int32, (images, rows), 1)
    image = lax.broadcasted_iota(jnp.int32, (images, rows), 0)
    inside = (token >= image * IMG_TOK) & (token < (image + 1) * IMG_TOK)
    return inside.astype(f32).astype(bf16)


def load_parts(parts, target, sems, col, col_count):
    depth = target.shape[0] // col_count
    copies = []
    for k, part in enumerate(parts):
        place = pl.multiple_of((col ^ k) * depth, depth)
        copies.append(pltpu.make_async_copy(part, target.at[pl.ds(place, depth)], sems.at[k]))
    return copies


def image_mix(tokens, gain_ref, bias_ref, qkv_block, between, out_weight, norm_ref, heads_ref, mixed_ref):
    rows, width = tokens.shape
    images = rows // IMG_TOK
    norm_ref[...] = layer_norm(tokens.astype(f32), gain_ref[0:1, :], bias_ref[0:1, :]).astype(bf16)

    @pl.loop(0, 3)
    def _(j):
        columns = pl.ds(pl.multiple_of(j * width, width), width)
        heads_ref[:, columns] = dot_nn(norm_ref[...], qkv_block(j)).astype(bf16)

    between()
    first, second = lane_halves(128)
    factor = (width // HEADS) ** -0.5
    window = 112

    @pl.loop(0, images // 2)
    def _(pair):
        start = pair * (2 * IMG_TOK)
        low = pl.multiple_of(start // 16 * 16, 16)
        near = lax.broadcasted_iota(jnp.int32, (window, window), 0) + low
        far = lax.broadcasted_iota(jnp.int32, (window, window), 1) + low
        same = (near >= start) & (near < start + 2 * IMG_TOK) & (far >= start) & (far < start + 2 * IMG_TOK)
        same = same & ((near >= start + IMG_TOK) == (far >= start + IMG_TOK))
        bias = jnp.where(same, 0.0, masked_score)
        bias = jnp.concatenate([bias, bias], axis=0)
        keep = lax.broadcasted_iota(jnp.int32, (16, 128), 0) + low < start
        span, head, tail = pl.ds(low, window), pl.ds(low, 16), pl.ds(low + 16, window - 16)
        for at in range(0, width, 128):
            query = stack_heads(heads_ref[span, at : at + 128], first, second)
            key = heads_ref[span, width + at : width + at + 128]
            weights, scale = soft_weights(query, key, bias, factor)
            value = heads_ref[span, 2 * width + at : 2 * width + at + 128]
            mixed = join_heads(dot_nn(weights.astype(bf16), value) * scale)
            former = mixed_ref[head, at : at + 128].astype(f32)
            mixed_ref[head, at : at + 128] = jnp.where(keep, former, mixed[:16]).astype(bf16)
            mixed_ref[tail, at : at + 128] = mixed[16:].astype(bf16)

    mid = tokens.astype(f32) + dot_nn(mixed_ref[...], out_weight())
    high, low = split_low(mid)
    select = group_mean(images, rows)
    mean = (dot_nn(select, high) + dot_nn(select, low)) * (1.0 / IMG_TOK)
    return layer_norm(mid, gain_ref[1:2, :], bias_ref[1:2, :]).astype(bf16), mean


def image_mix_kernel(col_count, tok_ref, gain_ref, bias_ref, *refs):
    qkv_parts, out_parts = refs[:col_count], refs[col_count : 2 * col_count]
    normed_ref, mean_ref, w_qkv, w_out, *buffers, sems = refs[2 * col_count :]
    col = lax.axis_index("col")

    @pl.when(pl.program_id(0) == 0)
    def _():
        copies = load_parts(qkv_parts, w_qkv, sems.at[0], col, col_count)
        copies += load_parts(out_parts, w_out, sems.at[1], col, col_count)
        for copy in copies:
            copy.start()
        for copy in copies:
            copy.wait()

    width = tok_ref.shape[1]

    def qkv_block(j):
        return w_qkv[:, pl.ds(pl.multiple_of(j * width, width), width)]

    normed_ref[...], mean_ref[...] = image_mix(
        tok_ref[...], gain_ref, bias_ref, qkv_block, lambda: None, lambda: w_out[...], *buffers
    )


def image_embed_kernel(col_count, normed_ref, mean_ref, *refs):
    up_parts, down_parts = refs[:col_count], refs[col_count : 2 * col_count]
    embed_ref, w_up, w_down, sum_ref, sems = refs[2 * col_count :]
    rows, width = normed_ref.shape
    images = rows // IMG_TOK
    wide = w_up.shape[1]
    step = pl.program_id(0)
    col = lax.axis_index("col")
    downs = load_parts(down_parts, w_down, sems.at[1], col, col_count)

    @pl.when(step == 0)
    def _():
        ups = load_parts(up_parts, w_up, sems.at[0], col, col_count)
        for copy in ups + downs:
            copy.start()
        for copy in ups:
            copy.wait()

    select = group_mean(images, rows)

    @wide_steps(wide)
    def _(columns):
        inner = gelu(dot_nn(normed_ref[...], w_up[:, columns])).astype(bf16)
        sum_ref[pl.ds(pl.multiple_of(step * images, images), images), columns] = dot_nn(select, inner)

    @pl.when(step == pl.num_programs(0) - 1)
    def _():
        for copy in downs:
            copy.wait()
        high, low = split_low(sum_ref[...] * (1.0 / IMG_TOK))
        pooled = mean_ref[...] + dot_nn(high, w_down[...]) + dot_nn(low, w_down[...])
        embed_ref[...] = (
            pooled * lax.rsqrt(jnp.sum(pooled * pooled, axis=-1, keepdims=True) + norm_eps)
        ).astype(bf16)


joined_ins = (
    "lengths", "gain1", "bias1", "gain2", "bias2", "image_gain", "image_bias", "tok_hbm", "qkv_hbm", "out_hbm",
    "up_hbm", "down_hbm", "proj_hbm", "image_hbm", "image_qkv_hbm", "image_out_hbm", "image_up_hbm",
    "image_down_hbm",
)
joined_outs = (
    "up_out", "out_out", "qkv_out", "down_out", "proj_out", "norm_out", "hidden_out", "input_out", "slope_out",
)


def joined_kernel(names, *refs):
    refs = dict(zip(joined_ins + joined_outs + names, refs, strict=True))
    tok_load = pltpu.make_async_copy(refs["tok_hbm"], refs["tok"], refs["tok_sems"].at[2])
    tok_load.start()
    t = TextForward(refs)
    place = Place()
    place.greet()
    groups, group_rows = t.image_hbm.shape[0] // t.image_tok.shape[1], t.image_tok.shape[1]
    group_images = group_rows // IMG_TOK
    width, cols = t.width, place.cols

    def load_group(group):
        span = pl.ds(pl.multiple_of(group * group_rows, 16), group_rows)
        slot = group % 2
        return pltpu.make_async_copy(t.image_hbm.at[span], t.image_tok.at[slot], t.tok_sems.at[slot])

    load_group(0).start()
    gathers = iter(range(t.sends.shape[0]))

    def gather(pieces, *spans):
        i = next(gathers)
        return Gather(place, pieces, spans, t.sends.at[i], t.recvs.at[i])

    def piece_of_columns(axis, shard, at, target):
        lanes = pl.ds(at, target.shape[-1])
        return (
            axis, shard.at[:, :, lanes], lambda half: shard.at[half, :, lanes],
            lambda col: target.at[col], lambda col, half: target.at[col, half],
        )

    qkv_gathers = [
        gather(
            [piece_of_columns("y", t.image_qkv_hbm, j * width, t.iw_qkv.at[j])], t.iw_qkv.at[j, 0], t.iw_qkv.at[j, 0, 0]
        )
        for j in range(3)
    ]
    out_piece = (
        "z", t.image_out_hbm, lambda half: t.image_out_hbm.at[half],
        lambda col: t.iw_out.at[col // 2, pl.ds(col % 2 * 2, 2)],
        lambda col, half: t.iw_out.at[col // 2, col % 2 * 2 + half],
    )
    out_gather = gather([out_piece], t.iw_out.at[0, pl.ds(0, 2)], t.iw_out.at[0, 0])
    up_pieces = [
        piece_of_columns("yzyz"[j], t.image_up_hbm, j * width, t.iw_up.at[j // 2, j % 2]) for j in range(4)
    ]
    up_gather = gather(up_pieces, t.iw_up.at[0, 0], t.iw_up.at[0, 0, pl.ds(0, 2)])

    def piece_of_down(axis, lanes):
        return (
            axis, t.image_down_hbm.at[:, :, :, lanes],
            lambda half: t.image_down_hbm.at[pl.ds(half * 2, 2), :, :, lanes],
            lambda col: t.iw_down.at[col // 2, col % 2, :, :, :, lanes],
            lambda col, half: t.iw_down.at[col // 2, col % 2, pl.ds(half * 2, 2), :, :, lanes],
        )

    down_pieces = [piece_of_down("yz"[j], pl.ds(j * width // 2, width // 2)) for j in range(2)]
    down_gather = gather(down_pieces, t.iw_down.at[0, 0], t.iw_down.at[0, 0, pl.ds(0, 2)])

    def each(pieces, step):
        for piece in pieces:
            getattr(piece, step)()

    factors, pooled_factors = (
        RowFactors(
            place, getattr(t, "own" + tag), getattr(t, "held" + tag), t.factor_local.at[i], t.factor_sends.at[i],
            t.factor_recvs.at[i],
        )
        for i, tag in enumerate(("_inner", "_pooled"))
    )
    saves = {
        name: pltpu.make_async_copy(refs[name], refs[name + "_out"], t.save_sems.at[i])
        for i, name in enumerate(("hidden", "slope"))
    }
    tok_load.wait()
    t.prepare()
    place.meet()
    each(qkv_gathers, "start")
    out_gather.start()
    t.attention()
    qkv_gathers[0].share()
    t.middle()

    def after_feed(j):
        pl.when(j == 0)(qkv_gathers[1].share)
        pl.when(j == 1)(qkv_gathers[2].share)

        @pl.when(j == 2)
        def _():
            out_gather.share()
            up_gather.start()

    t.feed(after_feed)
    saves["slope"].start()
    inner_step = t.wide // place.rows
    for row in range(place.rows):
        t.own_inner[row] = t.inner_sum[:, row * inner_step : (row + 1) * inner_step]
    each(qkv_gathers, "relay")
    each(qkv_gathers, "finish")
    saves["slope"].wait()

    image_norm, image_mixed = t.w_out.at[pl.ds(0, group_rows)], t.w_proj.at[pl.ds(0, group_rows)]
    image_heads = t.w_qkv.at[pl.ds(0, group_rows)]

    def normed_group(group):
        return t.slope.at[pl.ds(0, group_rows), pl.ds(pl.multiple_of(group * width, 128), width)]

    @pl.loop(0, groups)
    def _(group):
        @pl.when(group + 1 < groups)
        def _():
            load_group(group + 1).start()

        load_group(group).wait()

        def between():
            pl.when(group == 0)(out_gather.relay)
            pl.when(group == groups - 1)(down_gather.share)

        def out_weight():
            @pl.when(group == 0)
            def _():
                out_gather.finish()
                factors.start()

            return t.iw_out[...].reshape(width, width)

        normed2, mean = image_mix(
            t.image_tok[group % 2], t.image_gain, t.image_bias, lambda j: t.iw_qkv[j].reshape(width, width), between,
            out_weight, image_norm, image_heads, image_mixed,
        )
        normed_group(group)[...] = normed2
        t.image_mean[pl.ds(pl.multiple_of(group * group_images, 8), group_images), :] = mean

        @pl.when(group == 0)
        def _():
            down_gather.start()

        @pl.when(group == 1)
        def _():
            up_gather.share()

        @pl.when(group == 2)
        def _():
            up_gather.relay()

    again = (("w_out", t.out_hbm), ("w_qkv", t.qkv_hbm), ("slope", t.slope_out))
    again = {
        name: pltpu.make_async_copy(source, refs[name], t.again_sems.at[i]) for i, (name, source) in enumerate(again)
    }
    t.load_proj.start()
    again["w_out"].start()
    again["w_qkv"].start()
    up_gather.finish()

    halves, half_images = 2, t.own.shape[0] // 2
    half_groups = half_images // group_images
    corner = place.y * 2 + place.x

    def image_copies(half, stage):
        mine = t.near_qkv.at[half, corner, place.k, pl.ds(0, 4 * half_images)]
        own = mine.at[pl.ds(pl.multiple_of(place.z * half_images, 16), half_images)]

        def copy(n, block, **moved):
            return remote(block, block, t.image_sends.at[half, n], t.image_recvs.at[half, n], place.at(**moved))

        if stage == 0:
            return [copy(i - 1, own, z=(place.z + i) % 4) for i in range(1, 4)]
        if stage == 1:
            moves = ({"x": 1 - place.x}, {"y": 1 - place.y}, {"x": 1 - place.x, "y": 1 - place.y})
            return [copy(3 + i, mine, **move) for i, move in enumerate(moves)]
        held = t.near_qkv.at[half, :, place.k, pl.ds(0, 4 * half_images)]
        return [copy(6, held, k=1 - place.k)]

    def image_start(half, stage):
        for copy in image_copies(half, stage):
            copy.start()

    def image_finish(half, stage):
        for copy in image_copies(half, stage):
            copy.wait()

    select = group_mean(half_images, half_images * IMG_TOK)

    @pl.loop(0, halves)
    def _(half):
        @pl.loop(0, t.wide // width)
        def _(j):
            weight = t.iw_up[j // 2, j % 2].reshape(width, width)
            total = 0.0
            for group in range(half_groups):
                at = pl.ds(pl.multiple_of((half * half_groups + group) * width, 128), width)
                inner = gelu(dot_nn(t.slope[:group_rows, at], weight)).astype(bf16)
                total = total + dot_nn(select[:, group * group_rows : (group + 1) * group_rows], inner)
            t.sums[:, pl.ds(pl.multiple_of(j * width, 128), width)] = total

            @pl.when((half == 0) & (j == 1))
            def _():
                down_gather.relay()

            @pl.when((half == 1) & (j == 1))
            def _():
                image_finish(0, 0)
                image_start(0, 1)

        @pl.when(half == 0)
        def _():
            down_gather.finish()
            factors.share()

        pl.when(half == 1)(again["slope"].start)
        high, low = split_low(t.sums[...] * (1.0 / IMG_TOK))
        pooled = dot_nn(jnp.concatenate([high, low], axis=0), t.iw_down[...].reshape(t.wide, width))
        part = pl.ds(pl.multiple_of(half * half_images, 16), half_images)
        pooled = t.image_mean[part, :] + pooled[:half_images] + pooled[half_images:]
        embed = pooled * lax.rsqrt(jnp.sum(pooled * pooled, axis=-1, keepdims=True) + norm_eps)
        t.own[part, :] = embed.astype(bf16)
        span = pl.ds(pl.multiple_of(place.z * half_images, 16), half_images)
        t.near_qkv[half, corner, place.k, span] = embed.astype(bf16)
        image_start(half, 0)

    factors.relay()
    t.finish()
    saves["hidden"].start()
    image_finish(halves - 1, 0)
    image_start(halves - 1, 1)
    image_finish(0, 1)
    image_start(0, 2)
    t.embed()
    width_step = width // place.rows
    pooled = t.pooled[...]
    spare = jnp.zeros((t.captions, t.own_pooled.shape[2] - width_step), bf16)
    for row in range(place.rows):
        block = pooled[:, row * width_step : (row + 1) * width_step]
        t.own_pooled[row] = jnp.concatenate([block, spare], axis=1)
    factors.finish()
    image_finish(halves - 1, 1)
    image_start(halves - 1, 2)
    for half in range(halves):
        image_finish(half, 2)

    images = t.near_qkv[:, :, :, : 4 * half_images].reshape(-1, width)
    own = t.own[...].astype(f32)
    lifted = jnp.exp2(dot_nt(t.text_embed[...], images) * (logit_scale * log2e))
    t.own_sums[...] = jnp.sum(lifted, axis=0, keepdims=True)
    t.all_sums[place.slot] = t.own_sums[...]
    sums = Exchange(place, t.own_sums, t.all_sums, t.sum_sends, t.sum_recvs)
    sums.start()
    col_sums = jnp.sum(lifted, axis=1, keepdims=True)
    positives = logit_scale * jnp.sum(own * t.text_embed[...].astype(f32), axis=(0, 1), keepdims=True)
    logs = jnp.sum(jnp.log(col_sums), axis=(0, 1), keepdims=True)
    saves["hidden"].wait()
    pooled_factors.start()
    sums.finish()
    row_sums = jnp.sum(t.all_sums[...], axis=0)
    sim_grad = (0.5 * (lifted * (1.0 / row_sums) + lifted * (1.0 / col_sums))).astype(bf16)
    t.embed_grad[...] = logit_scale * (dot_nn(sim_grad, images) - own)
    logs = logs + jnp.sum(jnp.log(row_sums), axis=(0, 1), keepdims=True) * (1.0 / place.count)
    t.loss[...] = jnp.broadcast_to(0.5 * logs - positives, t.loss.shape)

    shared = {
        "low_grad": t.inner.at[:, pl.ds(3 * width, width)], "heads_grad": t.inner.at[:, pl.ds(0, 3 * width)],
        "mixed_grad": t.hidden, "key_column": t.outer.at[:, pl.ds(0, 128)],
    }
    backward(place, TextBackward(refs | shared, again), pooled_factors)


def backward(place, t, pooled_factors):
    width, cols = t.width, place.cols
    widths = scatter_widths(t.wide, width, cols)
    shared = {
        "_up": (
            t.iw_up, t.iw_qkv.at[pl.ds(0, 2)], t.iw_qkv.at[2, :, :, :, pl.ds(0, 384)], t.iw_out.at[:, :, :, pl.ds(0, 384)]
        ),
        "_qkv": (
            t.iw_down, t.near_qkv, t.iw_qkv.at[2, :, :, :, pl.ds(384, 384)], t.iw_out.at[:, :, :, pl.ds(384, 384)]
        ),
        "_outs": (
            t.iw_down.at[:, :, :, :, :, pl.ds(640, 128)], t.near_qkv.at[:, :, :, :, pl.ds(640, 128)],
            t.x1_outs, t.y1_outs,
        ),
    }
    up, out, qkv = (
        GradientScatter(
            place, tag == "_qkv", halves, *shared[tag], *(getattr(t, name + tag) for name in scatter_names)
        )
        for halves, tag in zip(widths, ("_up", "_outs", "_qkv"))
    )
    factors = ColFactors(place, t.own_cols, t.held_cols, t.col_sends, t.col_recvs)
    late, last = (
        ChipSum(place, *(getattr(t, name + tag) for name in total_names)) for tag in ("_late", "_last")
    )

    left = []

    def leave(name, ref):
        left.append(pltpu.make_async_copy(ref, getattr(t, name + "_out"), t.leave_sems.at[len(left)]))
        left[-1].start()

    def store(scatter, part, at, value):
        held = scatter.held
        size = value.shape[1]
        held[part // 2, part % 2, :, :, :, at : at + size] = value.reshape(*held.shape[2:5], size)

    def fill(scatter, chunk, total, block):
        at, size = scatter.lanes(chunk)[0].start, scatter.lanes(chunk)[0].size
        true = min(size, total // cols - at)
        for part in range(cols):
            start = part * (total // cols) + at
            store(scatter, part, at, block(slice(start, start + true)))

    def fill_up(chunk, between=lambda: None):
        at = up.lanes(chunk)[0].start
        size = up.lanes(chunk)[0].size
        for part in range(cols):
            start = part * up.held.shape[5] + at
            t.inner_grad(pl.ds(start, size))
        between()
        fill(up, chunk, t.wide, t.up_block)
        up.start(chunk, 0)

    proj_grad, branch = t.project()
    out_step = width // cols
    for part in range(cols):
        columns = slice(part * out_step, (part + 1) * out_step)
        t.own_cols[part] = jnp.concatenate([branch[:, columns], proj_grad[:, columns]], axis=1)
    t.held_cols[place.col, place.row] = t.own_cols[place.col]
    factors.start(0)
    pooled_factors.share()
    t.wait("slope")
    fill_up(0)
    fill_up(1)
    factors.finish(0)
    factors.start(1)
    up.step_on(0, 1)
    fill_up(2)
    up.step_on(1, 1)
    t.to_middle()
    factors.finish(1)
    factors.start(2)
    up.step_on(2, 1)
    pooled_factors.relay()
    t.middle()
    up.step_on(0, 2)
    for part in range(cols):
        value = t.out_block(slice(part * out_step, (part + 1) * out_step))
        store(out, part, 0, value[:, :128])
        store(qkv, part, 3 * out_step, value[:, 128:])
    out.start(0, 0)
    t.total_late[...] = jnp.concatenate([t.norm_grad[2:3, :], t.norm_grad[3:4, :], t.loss[...]], axis=1)
    late.start()
    t.to_heads()
    up.step_on(1, 2)
    out.step_on(0, 1)
    late.spread()

    def after(block):
        @pl.when(block == 0)
        def _():
            factors.finish(2)
            factors.start(3)

        @pl.when(block == 1)
        def _():
            up.step_on(2, 2)
            up.step_on(0, 3)

        @pl.when(block == 2)
        def _():
            up.step_on(1, 3)

    t.attention(after)
    fill(qkv, 0, 3 * width, t.qkv_block)
    qkv.start(0, 0)
    out.step_on(0, 2)
    fill(qkv, 1, 3 * width, t.qkv_block)
    qkv.start(1, 0)
    qkv.step_on(0, 1)
    fill(qkv, 2, 3 * width, t.qkv_block)
    qkv.start(2, 0)
    up.step_on(2, 3)
    qkv.step_on(1, 1)

    def between():
        up.step_on(0, 4)
        up.step_on(1, 4)
        qkv.step_on(0, 2)

    t.input(between)
    leave("input", t.tok)
    qkv.step_on(2, 1)
    out.step_on(0, 3)
    up.step_on(2, 4)
    t.total_last[...] = jnp.concatenate([t.norm_grad[0:1, :], t.norm_grad[1:2, :]], axis=1)
    last.start()
    qkv.step_on(0, 3)
    last.spread()
    factors.finish(3)
    pooled_factors.finish()
    col_factors = t.held_cols[...].reshape(-1, t.held_cols.shape[3])
    grown = dot_tn(col_factors, t.held_inner[...].reshape(-1, t.held_inner.shape[3]))
    t.down[...] = grown[:out_step]
    leave("down", t.down)
    grown = dot_tn(col_factors, t.held_pooled[...].reshape(-1, t.held_pooled.shape[3]))
    t.proj[...] = grown[out_step:].T[: width // place.rows]
    leave("proj", t.proj)
    qkv.step_on(1, 2)
    out.step_on(0, 4)
    qkv.step_on(2, 2)
    qkv.step_on(1, 3)
    t.norms[:, 2 * width :] = late.finish()
    qkv.step_on(2, 3)
    for chunk in range(len(up.halves)):
        up.finish(chunk, 4)
    t.up[...] = up.total()
    leave("up", t.up)
    t.norms[:, : 2 * width] = last.finish()
    leave("norm", t.norms)
    out.finish(0, 4)
    t.out[:, :128] = out.total()
    for chunk in range(len(qkv.halves)):
        qkv.finish(chunk, 3)
    total = qkv.total()
    t.qkv[...] = total[:, : 3 * out_step]
    leave("qkv", t.qkv)
    t.out[:, 128:] = total[:, 3 * out_step : 4 * out_step - 128]
    leave("out", t.out)
    for copy in left:
        copy.wait()


def whole(shape):
    return pl.BlockSpec(shape, lambda *_: (0,) * len(shape))


in_vmem = pl.BlockSpec(memory_space=pltpu.VMEM)
in_smem = pl.BlockSpec(memory_space=pltpu.SMEM)
anywhere = pl.BlockSpec(memory_space=pl.ANY)


def plain(kernel, outs, ins, scratch, name, out_specs=None, **settings):
    return pl.pallas_call(
        kernel,
        out_shape=outs,
        in_specs=ins,
        out_specs=out_specs or [in_vmem] * len(outs),
        scratch_shapes=scratch,
        compiler_params=pltpu.CompilerParams(vmem_limit_bytes=VMEM_LIMIT, **settings),
        name=name,
    )


def array(shape, dtype):
    return jax.ShapeDtypeStruct(shape, dtype)


def partners(x, col_count):
    order = [(i, i ^ 2) for i in range(col_count)]
    near = [(i, i ^ 1) for i in range(col_count)]
    far = lax.ppermute(x, "col", order)
    return [x, lax.ppermute(x, "col", near), far, lax.ppermute(far, "col", near)]


def body(
    image_tokens, image_norm_gain, image_norm_bias, image_qkv, image_out, image_up, image_down,
    text_tokens, text_lengths, norm1_gain, norm1_bias, norm2_gain, norm2_bias,
    text_qkv, text_out, text_up, text_down, text_proj,
):
    tokens, width = text_tokens.shape
    captions = text_lengths.shape[0]
    length = tokens // captions
    wide = text_up.shape[1]
    row_count, col_count = lax.axis_size("row"), lax.axis_size("col")
    row, col = lax.axis_index("row"), lax.axis_index("col")
    pair_total = captions * row_count * col_count
    image_rows, images = image_tokens.shape[0], image_tokens.shape[0] // IMG_TOK

    count = row_count * col_count
    joined = (row_count, col_count) == (8, 4)
    vectors = (norm1_gain, norm1_bias, norm2_gain, norm2_bias)
    weights = (text_qkv, text_out, text_up, text_down, text_proj)
    weight_scratch = [pltpu.VMEM(w.shape, bf16) for w in weights]

    text_shapes = (
        array((tokens, width), bf16),
        array((captions, width), bf16),
        array((captions, width), f32),
        array((captions, width), bf16),
        array((captions, wide), bf16),
        array((tokens, 3 * width), bf16),
        array((tokens, width), bf16),
        array((tokens, width), f32),
        array((tokens, wide), bf16),
        array((width, tokens), bf16),
    )
    text_specs = [in_vmem, in_smem] + [in_vmem] * 4 + [anywhere] * 5
    text_buffers = weight_scratch + [
        pltpu.VMEM((tokens, width), bf16),
        pltpu.VMEM((tokens, wide), bf16),
        pltpu.VMEM((captions, 1), jnp.int32),
        pltpu.VMEM((1, tokens), f32),
        pltpu.SemaphoreType.DMA((5,)),
    ]
    text_in = (text_tokens, text_lengths, *vectors, *weights)
    groups = 4
    group_rows, group_images = image_rows // groups, images // groups
    mix_buffers = [
        pltpu.VMEM((group_rows, width), bf16),
        pltpu.VMEM((group_rows, 3 * width), bf16),
        pltpu.VMEM((group_rows, width), bf16),
    ]
    mix_weights = [pltpu.VMEM((width, 3 * width), bf16), pltpu.VMEM((width, width), bf16)]
    embed_weights = [pltpu.VMEM((width, wide), bf16), pltpu.VMEM((wide, width), bf16)]
    both = ("row", "col")

    if joined:
        halves, rows = 2, width // row_count
        out_step, inner_step = width // col_count, wide // row_count
        packed = -(-rows // 128) * 128
        dma = pltpu.SemaphoreType.DMA
        widths = scatter_widths(wide, width, col_count)
        sets = {tag: scatter_scratch(rows, each) for each, tag in zip(widths, ("_up", "_outs", "_qkv"))}
        scratch = dict(zip(text_names, (pltpu.VMEM(shape.shape, shape.dtype) for shape in text_shapes)))
        scratch |= dict(zip(text_scratch, text_buffers))
        scratch |= {
            "tok": pltpu.VMEM((tokens, width), bf16),
            "iw_qkv": pltpu.VMEM((3, 4, 2, rows, width), bf16),
            "iw_out": pltpu.VMEM((2, 4, rows, width), bf16),
            "iw_up": pltpu.VMEM((2, 2, 4, 2, rows, width), bf16),
            "iw_down": pltpu.VMEM((2, 2, 4, 2, rows, width), bf16),
            "image_tok": pltpu.VMEM((2, group_rows, width), bf16),
            "image_mean": pltpu.VMEM((images, width), f32),
            "sums": pltpu.VMEM((images // halves, wide), f32),
            "own": pltpu.VMEM((images, width), bf16),
            "own_inner": pltpu.VMEM((row_count, captions, inner_step), bf16),
            "held_inner": pltpu.VMEM((col_count, row_count, captions, inner_step), bf16),
            "own_pooled": pltpu.VMEM((row_count, captions, packed), bf16),
            "held_pooled": pltpu.VMEM((col_count, row_count, captions, packed), bf16),
            "up": pltpu.VMEM((rows, wide // col_count), f32),
            "out": pltpu.VMEM((rows, out_step), f32),
            "qkv": pltpu.VMEM((rows, 3 * out_step), f32),
            "down": pltpu.VMEM((out_step, inner_step), f32),
            "proj": pltpu.VMEM((rows, out_step), f32),
            "norms": pltpu.VMEM((1, 4 * width + 128), f32),
            "leave_sems": dma((7,)),
            "own_sums": pltpu.VMEM((1, pair_total), f32),
            "all_sums": pltpu.VMEM((count, 1, pair_total), f32),
            "tok_sems": dma((3,)),
            "again_sems": dma((3,)),
            "save_sems": dma((2,)),
            "sends": dma((6, 4)),
            "recvs": dma((6, 5)),
            "factor_local": dma((2,)),
            "factor_sends": dma((2, 4)),
            "factor_recvs": dma((2, 4)),
            "image_sends": dma((halves, 7)),
            "image_recvs": dma((halves, 7)),
            "sum_sends": dma((1,)),
            "sum_recvs": dma((1,)),
            "embed_grad": pltpu.VMEM((captions, width), f32),
            "loss": pltpu.VMEM((1, 128), f32),
            "branch": pltpu.VMEM((captions, width), bf16),
            "norm_grad": pltpu.VMEM((8, width), f32),
            "outer": pltpu.VMEM((tokens, width), f32),
            "mid_grad": pltpu.VMEM((tokens, width), f32),
            "near_qkv": pltpu.VMEM((2, 4, 2, rows, width), bf16),
            "own_cols": pltpu.VMEM((col_count, captions, 2 * out_step), bf16),
            "held_cols": pltpu.VMEM((col_count, row_count, captions, 2 * out_step), bf16),
            "col_sends": dma((7,)),
            "col_recvs": dma((7,)),
        }
        scratch |= dict(zip(("x1_outs", "y1_outs"), sets["_outs"][2:]))
        for tag, buffers in sets.items():
            scratch |= {name + tag: buffer for name, buffer in zip(scatter_names, buffers[4:])}
        for tag, size in (("_late", 2 * width + 128), ("_last", 2 * width)):
            scratch |= {name + tag: buffer for name, buffer in zip(total_names, chip_sum_scratch(size, count // 2))}
        up_grad, out_grad, qkv_grad, grad_down, grad_proj, norm_total, hidden, input_grad, _ = plain(
            functools.partial(joined_kernel, tuple(scratch)),
            (
                array((rows, wide // col_count), f32),
                array((rows, out_step), f32),
                array((rows, 3 * out_step), f32),
                array((out_step, inner_step), f32),
                array((rows, out_step), f32),
                array((1, 4 * width + 128), f32),
                array((tokens, width), bf16),
                array((tokens, width), bf16),
                array((tokens, wide), bf16),
            ),
            [in_smem] + [in_vmem] * 6 + [anywhere] * 11,
            list(scratch.values()),
            "joined",
            out_specs=[anywhere] * 9,
            collective_id=1,
            has_side_effects=True,
        )(
            text_lengths, *vectors, image_norm_gain, image_norm_bias, text_tokens, *weights, image_tokens,
            image_qkv.reshape(2, rows, -1), image_out.reshape(2, rows, -1), image_up.reshape(2, rows, -1),
            image_down.reshape(4, 2, rows, -1),
        )
        large = (hidden, input_grad, qkv_grad, out_grad, up_grad, grad_down, grad_proj)
        results = (array((1, 1), f32), *[array((width,), f32)] * 4, *(array(g.shape, g.dtype) for g in large))
        loss, *rest = plain(
            functools.partial(hand_over_kernel, pair_total), results, [in_vmem] * 8, [], "hand_over"
        )(norm_total, *large)
        norms, (hidden, input_grad, qkv_grad, out_grad, up_grad, grad_down, grad_proj) = rest[:4], rest[4:]
        return (
            loss.reshape(()), hidden, input_grad, *norms, qkv_grad, out_grad, up_grad, grad_down.T, grad_proj,
        )

    (hidden, text_embed, projected, pooled, inner_sum, heads, mixed, mid, slope, turned) = plain(
        text_forward_kernel, text_shapes, text_specs, text_buffers, "text_forward"
    )(*text_in)
    qkv_parts = partners(image_qkv, col_count)
    out_parts = partners(image_out, col_count)
    up_parts = partners(image_up, col_count)
    down_parts = partners(image_down, col_count)
    parts = [anywhere] * (2 * col_count)
    image_normed, image_mean = pl.pallas_call(
        functools.partial(image_mix_kernel, col_count),
        grid=(groups,),
        out_shape=(array((image_rows, width), bf16), array((images, width), f32)),
        in_specs=[
            pl.BlockSpec((group_rows, width), lambda i: (i, 0)),
            whole(image_norm_gain.shape),
            whole(image_norm_bias.shape),
        ]
        + parts,
        out_specs=(
            pl.BlockSpec((group_rows, width), lambda i: (i, 0)),
            pl.BlockSpec((group_images, width), lambda i: (i, 0)),
        ),
        scratch_shapes=mix_weights + mix_buffers + [pltpu.SemaphoreType.DMA((2, col_count))],
        compiler_params=pltpu.CompilerParams(vmem_limit_bytes=VMEM_LIMIT),
        name="image_mix",
    )(image_tokens, image_norm_gain, image_norm_bias, *qkv_parts, *out_parts)
    image_embed = pl.pallas_call(
        functools.partial(image_embed_kernel, col_count),
        grid=(groups,),
        out_shape=array((images, width), bf16),
        in_specs=[pl.BlockSpec((group_rows, width), lambda i: (i, 0)), whole((images, width))] + parts,
        out_specs=whole((images, width)),
        scratch_shapes=embed_weights
        + [pltpu.VMEM((images, wide), f32), pltpu.SemaphoreType.DMA((2, col_count))],
        compiler_params=pltpu.CompilerParams(vmem_limit_bytes=VMEM_LIMIT),
        name="image_embed",
    )(image_normed, image_mean, *up_parts, *down_parts)

    image_all = lax.all_gather(image_embed, both, axis=0, tiled=True)
    lifted = jnp.exp(logit_scale * dot_nt(image_all, text_embed))
    row_sums = lax.psum(jnp.sum(lifted, axis=1), both)
    col_sums = jnp.sum(lifted, axis=0)
    sim_grad = (0.5 * (lifted / row_sums[:, None] + lifted / col_sums[None, :])).astype(bf16)
    image_own = image_embed.astype(f32)
    embed_grad = logit_scale * (dot_tn(sim_grad, image_all) - image_own)
    positives = logit_scale * jnp.sum(image_own * text_embed.astype(f32), axis=1)
    loss_part = 0.5 * jnp.sum(jnp.log(col_sums) - 2.0 * positives)
    loss_part = loss_part + 0.5 * jnp.sum(jnp.log(row_sums)) / count

    saved = (text_tokens, heads, mixed, mid, slope, turned)
    backward_in = (text_lengths, *vectors, embed_grad, projected, *saved, *weights)
    backward_specs = [in_smem] + [in_vmem] * 6 + [anywhere] * 11
    backward_buffers = (
        [
            pltpu.VMEM((tokens, width), bf16),
            pltpu.VMEM((tokens, 3 * width), bf16),
            pltpu.VMEM((tokens, width), bf16),
            pltpu.VMEM((tokens, width), f32),
            pltpu.VMEM((tokens, wide), bf16),
        ]
        + weight_scratch
        + [
            pltpu.VMEM((tokens, width), bf16),
            pltpu.VMEM((width, tokens), bf16),
            pltpu.VMEM((tokens, width), f32),
            pltpu.VMEM((tokens, width), f32),
            pltpu.VMEM((tokens, width), bf16),
            pltpu.VMEM((tokens, width), bf16),
            pltpu.VMEM((tokens, 3 * width), bf16),
            pltpu.VMEM((captions, 1), jnp.int32),
            pltpu.VMEM((1, tokens), f32),
            pltpu.VMEM((tokens, 128), f32),
            pltpu.SemaphoreType.DMA((11,)),
        ]
    )

    def by_row(x):
        x = lax.all_to_all(x, "row", split_axis=1, concat_axis=0, tiled=True)
        return lax.all_gather(x, "col", axis=0, tiled=True)

    def by_col(x):
        x = lax.all_gather(x, "row", axis=0, tiled=True)
        return lax.all_to_all(x, "col", split_axis=1, concat_axis=0, tiled=True)

    (proj_grad, branch, up_grad, out_grad, qkv_grad, input_grad, norm_grads) = plain(
        text_backward_kernel,
        (
            array((captions, width), bf16),
            array((captions, width), bf16),
            array((col_count, width, wide // col_count), bf16),
            array((col_count, width, width // col_count), bf16),
            array((col_count, width, 3 * width // col_count), bf16),
            array((tokens, width), bf16),
            array((8, width), f32),
        ),
        backward_specs,
        backward_buffers,
        "text_backward",
    )(*backward_in)

    def scattered(matrix):
        blocks = matrix.reshape(count, width // row_count, matrix.shape[2])
        return lax.psum_scatter(blocks, ("col", "row"), scatter_dimension=0, tiled=True)[0].astype(f32)

    up_grad, out_grad, qkv_grad = scattered(up_grad), scattered(out_grad), scattered(qkv_grad)
    grad_down = dot_tn(by_row(inner_sum), by_col(branch))
    grad_proj = dot_tn(by_row(pooled), by_col(proj_grad))
    loss_total, norm_total = lax.psum((loss_part, norm_grads), both)
    norms = [norm_total[i] for i in range(4)]
    mean_loss = loss_total / pair_total
    return (
        mean_loss, hidden, input_grad, *norms, qkv_grad, out_grad, up_grad, grad_down, grad_proj,
    )


def solution(mesh):
    split = P(("row", "col"), None)
    grid = P("row", "col")
    in_specs = (
        split, P(), P(), P("col", None), P("col", None), P("col", None), P("col", None), split, P(("row", "col")),
    ) + (P(),) * 9
    out_specs = (P(), split, split, P(), P(), P(), P(), grid, grid, grid, grid, grid)
    return jax.shard_map(body, mesh=mesh, in_specs=in_specs, out_specs=out_specs, check_vma=False)
```

profile of v0, /device:TPU:0, one launch (start us, length us, event | category | flops | bytes accessed | tf_op | source)
XLA Modules:
  0.0 157.6 jit_solution(6534669939546653605)
XLA Ops:
  0.7 153.7 %joined.1 = (f32[96,768]{1,0:T(8,128)}, f32[96,192]{1,0:T(8,128)}, f32[96,576]{1,0:T(8,128)}, f32[192,384]{1,0:T(8,128)}, f32[96,192]{1,0:T(8,128)}, /*index=5*/...) custom-call(s32[32]{0:T(128)} %refs_0_.1, f32[768]{0:T(1024)} %refs_1_.1, ...), custom_call_target="tpu_custom_call" | custom-call | tf_op jit(solution)/shard_map/joined/pallas_call | solution.py:1505
  154.4 3.2 %hand_over.1 = (f32[1,1]{1,0:T(1,128)}, f32[768]{0:T(1024)}, f32[768]{0:T(1024)}, f32[768]{0:T(1024)}, f32[768]{0:T(1024)}, /*index=5*/bf16[512,768]{1,0:T(8,128...) custom-call(f32[1,3200]{1,0:T(1,128)} %get-tuple-element.32.norms, ...), custom_call_target="tpu_custom_call" | custom-call | tf_op jit(solution)/shard_map/hand_over/pallas_call | solution.py:1531
where the time goes:
time: 158 us
  Pallas kernels  157 us (99%)
    pallas_call x1, Pallas kernels, body(): plain(functools.partial(joined_kernel, tuple(scratch)), (array((rows, wid...  154 us
    pallas_call x1, Pallas kernels, body(): plain(functools.partial(hand_over_kernel, pair_total), results, [in_vmem]...  3.21 us

commit v1 on v0

--- a/solution.py
+++ b/solution.py
@@ -1017,14 +1017,15 @@
         def _():
             out_gather.share()
             up_gather.start()
+            qkv_gathers[0].relay()
+
+        pl.when(j == 3)(qkv_gathers[1].relay)
 
     t.feed(after_feed)
     saves["slope"].start()
     inner_step = t.wide // place.rows
     for row in range(place.rows):
         t.own_inner[row] = t.inner_sum[:, row * inner_step : (row + 1) * inner_step]
-    each(qkv_gathers, "relay")
-    each(qkv_gathers, "finish")
     saves["slope"].wait()
 
     image_norm, image_mixed = t.w_out.at[pl.ds(0, group_rows)], t.w_proj.at[pl.ds(0, group_rows)]
@@ -1041,9 +1042,19 @@
 
         load_group(group).wait()
 
+        def qkv_block(j):
+            pl.when((group == 0) & (j == 0))(qkv_gathers[2].relay)
+            for i, weight in enumerate(qkv_gathers):
+                pl.when((group == 0) & (j == i))(weight.finish)
+            return t.iw_qkv[j].reshape(width, width)
+
         def between():
             pl.when(group == 0)(out_gather.relay)
-            pl.when(group == groups - 1)(down_gather.share)
+
+            @pl.when(group == groups - 1)
+            def _():
+                up_gather.relay()
+                down_gather.share()
 
         def out_weight():
             @pl.when(group == 0)
@@ -1054,7 +1065,7 @@
             return t.iw_out[...].reshape(width, width)
 
         normed2, mean = image_mix(
-            t.image_tok[group % 2], t.image_gain, t.image_bias, lambda j: t.iw_qkv[j].reshape(width, width), between,
+            t.image_tok[group % 2], t.image_gain, t.image_bias, qkv_block, between,
             out_weight, image_norm, image_heads, image_mixed,
         )
         normed_group(group)[...] = normed2
@@ -1067,10 +1078,6 @@
         @pl.when(group == 1)
         def _():
             up_gather.share()
-
-        @pl.when(group == 2)
-        def _():
-            up_gather.relay()
 
     again = (("w_out", t.out_hbm), ("w_qkv", t.qkv_hbm), ("slope", t.slope_out))
     again = {
@@ -1085,28 +1092,42 @@
     half_groups = half_images // group_images
     corner = place.y * 2 + place.x
 
-    def image_copies(half, stage):
-        mine = t.near_qkv.at[half, corner, place.k, pl.ds(0, 4 * half_images)]
-        own = mine.at[pl.ds(pl.multiple_of(place.z * half_images, 16), half_images)]
-
-        def copy(n, block, **moved):
-            return remote(block, block, t.image_sends.at[half, n], t.image_recvs.at[half, n], place.at(**moved))
+    def image_block(half, z):
+        span = pl.ds(pl.multiple_of(z * half_images, 16), half_images)
+        return t.near_qkv.at[half, corner, place.k, span]
+
+    in_plane = ({"x": 1 - place.x}, {"y": 1 - place.y}, {"x": 1 - place.x, "y": 1 - place.y})
+
+    def image_start(half, stage):
+        def start(i, block, **moved):
+            sems = t.image_sends.at[half, i], t.image_recvs.at[half, i]
+            remote(block, block, *sems, place.at(**moved)).start()
 
         if stage == 0:
-            return [copy(i - 1, own, z=(place.z + i) % 4) for i in range(1, 4)]
+            for i in range(1, 4):
+                start(0, image_block(half, place.z), z=(place.z + i) % 4)
+            for move in in_plane:
+                start(1, image_block(half, place.z), **move)
         if stage == 1:
-            moves = ({"x": 1 - place.x}, {"y": 1 - place.y}, {"x": 1 - place.x, "y": 1 - place.y})
-            return [copy(3 + i, mine, **move) for i, move in enumerate(moves)]
-        held = t.near_qkv.at[half, :, place.k, pl.ds(0, 4 * half_images)]
-        return [copy(6, held, k=1 - place.k)]
-
-    def image_start(half, stage):
-        for copy in image_copies(half, stage):
-            copy.start()
+            for i in range(1, 4):
+                for move in in_plane:
+                    start(2, image_block(half, (place.z + i) % 4), **move)
+        if stage == 2:
+            start(3, t.near_qkv.at[half, :, place.k, pl.ds(0, 4 * half_images)], k=1 - place.k)
 
     def image_finish(half, stage):
-        for copy in image_copies(half, stage):
-            copy.wait()
+        three, mate = pl.ds(0, 3 * half_images), place.at(k=1 - place.k)
+
+        def wait(i, span):
+            wait_all(span, t.image_sends.at[half, i], t.image_recvs.at[half, i], mate)
+
+        if stage == 0:
+            wait(0, t.near_qkv.at[half, 0, place.k, three])
+        if stage == 1:
+            wait(1, t.near_qkv.at[half, 0, place.k, three])
+            wait(2, t.near_qkv.at[half, pl.ds(0, 3), place.k, three])
+        if stage == 2:
+            wait(3, t.near_qkv.at[half, :, place.k, pl.ds(0, 4 * half_images)])
 
     select = group_mean(half_images, half_images * IMG_TOK)
 
@@ -1254,9 +1275,9 @@
         t.own_cols[part] = jnp.concatenate([branch[:, columns], proj_grad[:, columns]], axis=1)
     t.held_cols[place.col, place.row] = t.own_cols[place.col]
     factors.start(0)
-    pooled_factors.share()
     t.wait("slope")
     fill_up(0)
+    pooled_factors.share()
     fill_up(1)
     factors.finish(0)
     factors.start(1)
@@ -1481,8 +1502,8 @@
             "factor_local": dma((2,)),
             "factor_sends": dma((2, 4)),
             "factor_recvs": dma((2, 4)),
-            "image_sends": dma((halves, 7)),
-            "image_recvs": dma((halves, 7)),
+            "image_sends": dma((halves, 4)),
+            "image_recvs": dma((halves, 4)),
             "sum_sends": dma((1,)),
             "sum_recvs": dma((1,)),
             "embed_grad": pltpu.VMEM((captions, width), f32),

time: 158 us -> 155 us (0.981)
  Pallas kernels: 157 us -> 154 us
    pallas_call x1, Pallas kernels: 154 us -> 150 us  [body(): plain(functools.partial(joined_kernel, tuple(scratch)), (array((rows, wid...]
where the time goes in v1:
time: 155 us; the launch traced here: 154 us
  Pallas kernels  154 us (99%)
    pallas_call x1, Pallas kernels, body(): plain(functools.partial(joined_kernel, tuple(scratch)), (array((rows, wid...  150 us
    pallas_call x1, Pallas kernels, body(): plain(functools.partial(hand_over_kernel, pair_total), results, [in_vmem]...  3.21 us

profile of v1, /device:TPU:0, one launch (start us, length us, event | category | flops | bytes accessed | tf_op | source)
XLA Modules:
  0.0 154.3 jit_solution(6621754811392850222)
XLA Ops:
  0.7 150.4 %joined.1 = (f32[96,768]{1,0:T(8,128)}, f32[96,192]{1,0:T(8,128)}, f32[96,576]{1,0:T(8,128)}, f32[192,384]{1,0:T(8,128)}, f32[96,192]{1,0:T(8,128)}, /*index=5*/...) custom-call(s32[32]{0:T(128)} %refs_0_.1, f32[768]{0:T(1024)} %refs_1_.1, ...), custom_call_target="tpu_custom_call" | custom-call | tf_op jit(solution)/shard_map/joined/pallas_call | solution.py:1526
  151.0 3.2 %hand_over.1 = (f32[1,1]{1,0:T(1,128)}, f32[768]{0:T(1024)}, f32[768]{0:T(1024)}, f32[768]{0:T(1024)}, f32[768]{0:T(1024)}, /*index=5*/bf16[512,768]{1,0:T(8,128...) custom-call(f32[1,3200]{1,0:T(1,128)} %get-tuple-element.32.norms, ...), custom_call_target="tpu_custom_call" | custom-call | tf_op jit(solution)/shard_map/hand_over/pallas_call | solution.py:1552

commit v2 on v1

--- a/solution.py
+++ b/solution.py
@@ -588,8 +588,9 @@
 
 
 class ChipSum:
-    def __init__(self, place, total, got, slots, sends, recvs):
-        self.place, self.total, self.got, self.slots = place, total, got, slots
+    def __init__(self, place, total, got, slots, both, sends, recvs):
+        self.place, self.total, self.got, self.slots, self.both = place, total, got, slots, both
+        self.half = slots.shape[2]
         self.sends, self.recvs = sends, recvs
         self.chip, self.chips = place.row * 2 + place.x, place.rows * 2
         self.mate = place.at(k=1 - place.k)
@@ -603,17 +604,28 @@
     def spread(self):
         self.near().wait()
         self.total[...] = self.total[...] + self.got[...]
-        self.slots[self.chip] = self.total[...]
+        mine = pl.ds(pl.multiple_of(self.place.k * self.half, 128), self.half)
+        self.slots[self.chip] = self.total[:, mine]
 
         @pl.loop(1, self.chips)
         def _(distance):
             other = (self.chip + distance) % self.chips
             to = other // 2, other % 2 * 2 + self.place.k
-            remote(self.total, self.slots.at[self.chip], self.sends.at[1], self.recvs.at[1], to).start()
+            src, dst = self.total.at[:, mine], self.slots.at[self.chip]
+            remote(src, dst, self.sends.at[1], self.recvs.at[1], to).start()
+
+    def passed(self):
+        mine = self.both.at[self.place.k]
+        return remote(mine, mine, self.sends.at[2], self.recvs.at[2], self.mate)
+
+    def collect(self):
+        wait_all(self.slots.at[pl.ds(0, self.chips - 1)], self.sends.at[1], self.recvs.at[1], self.mate)
+        self.both[self.place.k] = jnp.sum(self.slots[...], axis=0)
+        self.passed().start()
 
     def finish(self):
-        wait_all(self.slots.at[pl.ds(0, self.chips - 1)], self.sends.at[1], self.recvs.at[1], self.mate)
-        return jnp.sum(self.slots[...], axis=0)
+        self.passed().wait()
+        return jnp.concatenate([self.both[0], self.both[1]], axis=1)
 
 
 class GradientScatter:
@@ -730,8 +742,8 @@
 
 def chip_sum_scratch(size, chips):
     return [
-        pltpu.VMEM((1, size), f32), pltpu.VMEM((1, size), f32), pltpu.VMEM((chips, 1, size), f32),
-        pltpu.SemaphoreType.DMA((2,)), pltpu.SemaphoreType.DMA((2,)),
+        pltpu.VMEM((1, size), f32), pltpu.VMEM((1, size), f32), pltpu.VMEM((chips, 1, size // 2), f32),
+        pltpu.VMEM((2, 1, size // 2), f32), pltpu.SemaphoreType.DMA((3,)), pltpu.SemaphoreType.DMA((3,)),
     ]
 
 
@@ -784,7 +796,7 @@
 
 
 scatter_names = ("x2", "y2", "far", "sends", "recvs")
-total_names = ("total", "got", "slots", "sends", "recvs")
+total_names = ("total", "got", "slots", "both", "sends", "recvs")
 
 
 def hand_over_kernel(pair_total, norms, *refs):
@@ -1296,7 +1308,7 @@
         store(out, part, 0, value[:, :128])
         store(qkv, part, 3 * out_step, value[:, 128:])
     out.start(0, 0)
-    t.total_late[...] = jnp.concatenate([t.norm_grad[2:3, :], t.norm_grad[3:4, :], t.loss[...]], axis=1)
+    t.total_late[...] = jnp.concatenate([t.norm_grad[2:3, :], t.norm_grad[3:4, :], t.loss[...], t.loss[...]], axis=1)
     late.start()
     t.to_heads()
     up.step_on(1, 2)
@@ -1337,6 +1349,7 @@
 
     t.input(between)
     leave("input", t.tok)
+    late.collect()
     qkv.step_on(2, 1)
     out.step_on(0, 3)
     up.step_on(2, 4)
@@ -1357,8 +1370,9 @@
     out.step_on(0, 4)
     qkv.step_on(2, 2)
     qkv.step_on(1, 3)
-    t.norms[:, 2 * width :] = late.finish()
+    t.norms[:, 2 * width :] = late.finish()[:, : 2 * width + 128]
     qkv.step_on(2, 3)
+    last.collect()
     for chunk in range(len(up.halves)):
         up.finish(chunk, 4)
     t.up[...] = up.total()
@@ -1521,7 +1535,7 @@
         scratch |= dict(zip(("x1_outs", "y1_outs"), sets["_outs"][2:]))
         for tag, buffers in sets.items():
             scratch |= {name + tag: buffer for name, buffer in zip(scatter_names, buffers[4:])}
-        for tag, size in (("_late", 2 * width + 128), ("_last", 2 * width)):
+        for tag, size in (("_late", 2 * width + 256), ("_last", 2 * width)):
             scratch |= {name + tag: buffer for name, buffer in zip(total_names, chip_sum_scratch(size, count // 2))}
         up_grad, out_grad, qkv_grad, grad_down, grad_proj, norm_total, hidden, input_grad, _ = plain(
             functools.partial(joined_kernel, tuple(scratch)),

time: 155 us -> 153 us (0.987)
  Pallas kernels: 154 us -> 152 us
where the time goes in v2:
time: 153 us
  Pallas kernels  152 us (99%)
    pallas_call x1, Pallas kernels, body(): plain(functools.partial(joined_kernel, tuple(scratch)), (array((rows, wid...  149 us
    pallas_call x1, Pallas kernels, body(): plain(functools.partial(hand_over_kernel, pair_total), results, [in_vmem]...  3.21 us

profile of v2, /device:TPU:0, one launch (start us, length us, event | category | flops | bytes accessed | tf_op | source)
XLA Modules:
  0.0 153.2 jit_solution(16753344343186330924)
XLA Ops:
  0.7 149.3 %joined.1 = (f32[96,768]{1,0:T(8,128)}, f32[96,192]{1,0:T(8,128)}, f32[96,576]{1,0:T(8,128)}, f32[192,384]{1,0:T(8,128)}, f32[96,192]{1,0:T(8,128)}, /*index=5*/...) custom-call(s32[32]{0:T(128)} %refs_0_.1, f32[768]{0:T(1024)} %refs_1_.1, ...), custom_call_target="tpu_custom_call" | custom-call | tf_op jit(solution)/shard_map/joined/pallas_call | solution.py:1540
  149.9 3.2 %hand_over.1 = (f32[1,1]{1,0:T(1,128)}, f32[768]{0:T(1024)}, f32[768]{0:T(1024)}, f32[768]{0:T(1024)}, f32[768]{0:T(1024)}, /*index=5*/bf16[512,768]{1,0:T(8,128...) custom-call(f32[1,3200]{1,0:T(1,128)} %get-tuple-element.32.norms, ...), custom_call_target="tpu_custom_call" | custom-call | tf_op jit(solution)/shard_map/hand_over/pallas_call | solution.py:1566
